TPU v7x, 512 devices: a whole 4x4x16 slice. The times are simulated.
512 devices in a mesh: seq: 128 (over z, x, y_hi), head: 4 (over y_lo, core).
Axes of the slice: x: 4, y: 4 (y_hi: 2, y_lo: 2; y = y_hi * 2 + y_lo), z: 16, core: 2. Of those that a mesh axis runs over, the one named last changes fastest.
Arguments:
- query_rows: bfloat16 [24576, 1536], P('seq', 'head'), may hold values from -64 to 64
- key_rows: bfloat16 [24576, 1536], P('seq', 'head'), may hold values from -4 to 4
- value_rows: bfloat16 [24576, 1536], P('seq', 'head'), may hold values from -6 to 6
- attention_out: bfloat16 [24576, 1536], P('seq', 'head'), may hold values from -4 to 4
- output_grad: bfloat16 [24576, 1536], P('seq', 'head'), may hold values from -6 to 6
- out_weight: bfloat16 [768, 768], P('head'), may hold values from -0.21875 to 0.21875
- reach_mask: int32 [128, 12], P('seq'), may hold values 0 or 1
Outputs:
- query_grad: bfloat16 [24576, 1536], P('seq', 'head')
- key_grad: bfloat16 [24576, 1536], P('seq', 'head')
- value_grad: bfloat16 [24576, 1536], P('seq', 'head')
All inputs are finite; a program needn't handle non-finite values. No bound on the sum of `reach_mask` on one device may be relied on, other than what follows from the above.
Results may differ from a plain program's by a relative error of at most 0.017.
Values may be sent and summed in bfloat16 or wider, within the bound.
A program may use at most 128 MiB of HBM per device.

v0:
```python
import jax
import jax.numpy as jnp
from jax import lax
from jax.experimental import pallas as pl
from jax.experimental.pallas import tpu as pltpu
from jax.sharding import PartitionSpec as P

MESH = pl.DeviceIdType.MESH
HDIM = 64
PLANE = 8
SLOTS = 13
DELTA = (0, -8, 8, -16, 16, -1, 1, -2, 2, -4, 4, -32, 32)
SCALING = HDIM**-0.5
EXP2_SCALE = SCALING * 1.4426950408889634
F32 = jnp.float32
BF16 = jnp.bfloat16


def mask_column(delta):
    return 2 * (abs(delta).bit_length() - 1) + (delta < 0)


def opposite(slot):
    return slot + 1 - 2 * ((slot + 1) % 2)


def slot_delta(slot):
    pair = (slot + 1) // 2
    power = (pair + 2) % 5 + 2 * (pair // 6)
    size = (1 + power % 2) * (1 + 3 * ((power // 2) % 2)) * (1 + 15 * (power // 4))
    return size * (1 - 2 * (slot % 2))


def dot_nt(left, right):
    return lax.dot_general(left, right, (((1,), (1,)), ((), ())), preferred_element_type=F32)


def dot_nn(left, right):
    return jnp.dot(left, right, preferred_element_type=F32)


def kernel(
    blocks,
    heads,
    q_ref,
    k_ref,
    v_ref,
    ao_ref,
    og_ref,
    w_ref,
    reach_ref,
    dq_ref,
    dk_ref,
    dv_ref,
    qbuf,
    gbuf,
    ogbuf,
    wide,
    ebuf,
    kfull,
    vfull,
    ktrans,
    delta_rows,
    stat_out,
    stat_in,
    fact_out,
    fact_in,
    part_out,
    part_in,
    dk_acc,
    dv_acc,
    dq_acc,
    q_send,
    q_recv,
    g_send,
    g_recv,
    og_send,
    og_recv,
    stat_send,
    stat_recv,
    fact_send,
    fact_recv,
    part_send,
    part_recv,
):
    pairs, width = q_ref.shape
    head_count = width // (2 * HDIM)
    me = lax.axis_index("seq")
    my_head = lax.axis_index("head")
    spot = lax.rem(me, PLANE)
    plane_start = me - spot

    def at(delta):
        return lax.rem(me + delta + blocks, blocks)

    def in_plane(delta):
        return plane_start + lax.rem(spot + delta + PLANE, PLANE)

    def head_at(step):
        return lax.rem(my_head + step, heads)

    barrier = pltpu.get_barrier_semaphore()
    for delta in DELTA[1:]:
        pl.semaphore_signal(barrier, inc=1, device_id=(at(delta), my_head), device_id_type=MESH)
    for delta in (-1, 1, -2, 2, 4):
        pl.semaphore_signal(barrier, inc=1, device_id=(in_plane(delta), my_head), device_id_type=MESH)
    for step in range(1, heads):
        pl.semaphore_signal(barrier, inc=1, device_id=(me, head_at(step)), device_id_type=MESH)

    lane = lax.broadcasted_iota(jnp.int32, (1, 2 * HDIM), 1)
    low = lane < HDIM
    low_f = low.astype(F32)
    low_b = low_f.astype(BF16)
    high_b = (1.0 - low_f).astype(BF16)

    def cols(head):
        return pl.ds(head * 2 * HDIM, 2 * HDIM)

    def doubled(tile):
        tile = tile.astype(F32)
        turned = pltpu.roll(tile, HDIM, 1)
        return jnp.concatenate([jnp.where(low, tile, turned), jnp.where(low, turned, tile)], axis=0)

    def spread(tile):
        return jnp.concatenate([tile * low_b, tile * high_b], axis=0)

    qbuf[0] = q_ref[...]
    ogbuf[my_head] = og_ref[...]

    pl.semaphore_wait(barrier, 17 + heads - 1)

    def remote(src, dst, send_sem, recv_sem, seq, head=None):
        return pltpu.make_async_remote_copy(
            src_ref=src,
            dst_ref=dst,
            send_sem=send_sem,
            recv_sem=recv_sem,
            device_id=(seq, my_head if head is None else head),
            device_id_type=MESH,
        )

    def move(buf, send, recv, src_slot, dst_slot, seq):
        return remote(buf.at[src_slot], buf.at[dst_slot], send.at[dst_slot], recv.at[dst_slot], seq)

    def slot_of(delta):
        return DELTA.index(delta)

    def send_own(buf, send, recv):
        move(buf, send, recv, 0, slot_of(-8), at(8)).start()
        move(buf, send, recv, 0, slot_of(8), at(-8)).start()

    def send_plane_own(buf, send, recv):
        for delta in (4, -4, 2, -2, 1, -1):
            inside = spot + delta < PLANE if delta > 0 else spot + delta >= 0

            @pl.when(inside)
            def _():
                move(buf, send, recv, 0, slot_of(-delta), in_plane(delta)).start()

    def relay_near(buf, send, recv, sign):
        source = slot_of(-8 * sign)
        move(buf, send, recv, source, slot_of(-16 * sign), at(8 * sign)).start()
        for size in (4, 2, 1):
            delta = size * sign
            inside = spot + delta < PLANE if delta > 0 else spot + delta >= 0

            @pl.when(jnp.logical_not(inside))
            def _():
                move(buf, send, recv, source, slot_of(-delta), in_plane(delta)).start()

    def relay_far(buf, send, recv, sign):
        move(buf, send, recv, slot_of(-16 * sign), slot_of(-32 * sign), at(16 * sign)).start()

    def wait_recv(buf, send, recv, slot):
        move(buf, send, recv, slot, slot, at(8)).wait_recv()

    def wait_send(buf, send, recv, slot):
        move(buf, send, recv, slot, slot, at(8)).wait_send()

    send_own(qbuf, q_send, q_recv)
    for step in range(1, heads):
        remote(
            ogbuf.at[my_head], ogbuf.at[my_head], og_send.at[step], og_recv.at[my_head], me, head_at(step)
        ).start()
    send_plane_own(qbuf, q_send, q_recv)

    for head in range(head_count):
        keys = doubled(k_ref[:, cols(head)])
        kfull[head] = keys.astype(BF16)
        ktrans[head] = jnp.transpose(keys)[:HDIM].astype(BF16)
        vfull[head] = doubled(v_ref[:, cols(head)]).astype(BF16)
        dk_acc[head] = jnp.zeros((2 * pairs, 2 * HDIM), F32)
        dv_acc[head] = jnp.zeros((2 * pairs, 2 * HDIM), F32)
    wide[...] = jnp.zeros(wide.shape, BF16)
    for head in range(head_count):
        rows = w_ref[pl.ds(head * HDIM, HDIM), :]
        for parity in range(2):
            wide[parity, pl.ds((head * 2 + parity) * HDIM, HDIM), :] = rows

    def grads_of_attention():
        for step in range(1, heads):
            other = head_at(step)
            remote(ogbuf.at[other], ogbuf.at[other], og_send.at[step], og_recv.at[other], me, other).wait_recv()
        total = jnp.zeros((pairs, width), F32)
        for chunk in range(heads):
            half = chunk % 2
            total = total + dot_nt(ogbuf[chunk], wide[chunk // 2, :, pl.ds(half * width, width)])
        grads = total.astype(BF16)
        gbuf[0] = grads
        product = grads.astype(F32) * ao_ref[...].astype(F32)
        column = lax.broadcasted_iota(jnp.int32, (1, width), 1)
        first = lax.rem(column, 2 * HDIM) < HDIM
        both = jnp.concatenate([jnp.where(first, product, 0.0), jnp.where(first, 0.0, product)], axis=0)
        top = both.astype(BF16)
        rest = (both - top.astype(F32)).astype(BF16)
        chooser = (
            lax.broadcasted_iota(jnp.int32, (8, width), 1) // (2 * HDIM)
            == lax.broadcasted_iota(jnp.int32, (8, width), 0)
        )
        chooser = chooser.astype(F32).astype(BF16)
        delta_rows[...] = dot_nt(chooser, top) + dot_nt(chooser, rest)

    def first_pass(slot, carry):
        @pl.when(slot > 0)
        def _():
            wait_recv(qbuf, q_send, q_recv, slot)

        for sign in (1, -1):

            @pl.when(slot == slot_of(-8 * sign))
            def _():
                relay_near(qbuf, q_send, q_recv, sign)

            @pl.when(slot == slot_of(-16 * sign))
            def _():
                relay_far(qbuf, q_send, q_recv, sign)

        @pl.when(slot == 5)
        def _():
            grads_of_attention()
            send_own(gbuf, g_send, g_recv)
            send_plane_own(gbuf, g_send, g_recv)

        tops, sums = [], []
        for head in range(head_count):
            queries = spread(qbuf[slot, :, cols(head)])
            scores = dot_nt(kfull[head], queries)
            top = jnp.max(scores, axis=0, keepdims=True)
            weights = jnp.exp2((scores - top) * EXP2_SCALE)
            tops.append(top)
            sums.append(jnp.sum(weights, axis=0, keepdims=True))
            ebuf[slot * head_count + head] = weights.astype(BF16)
        stat_out[slot] = jnp.concatenate(tops + tops[:1] + sums + sums[:1], axis=0)

        @pl.when(slot > 0)
        def _():
            there = opposite(slot)
            remote(
                stat_out.at[slot],
                stat_in.at[there],
                stat_send.at[slot],
                stat_recv.at[there],
                at(slot_delta(slot)),
            ).start()

        return carry

    lax.fori_loop(0, SLOTS, first_pass, 0)

    for sign in (1, -1):
        wait_recv(gbuf, g_send, g_recv, slot_of(-8 * sign))
        relay_near(gbuf, g_send, g_recv, sign)

    live = [None] + [reach_ref[0, mask_column(delta)] > 0 for delta in DELTA[1:]]
    for slot in range(1, SLOTS):
        wait_recv(stat_in, stat_send, stat_recv, slot)

    def stats(slot):
        both = stat_out[0] if slot == 0 else stat_in[slot]
        return both[0:4], both[4:8]

    highest = stats(0)[0]
    for slot in range(1, SLOTS):
        highest = jnp.maximum(highest, jnp.where(live[slot], stats(slot)[0], -1e30))
    ratios = []
    total = jnp.zeros(highest.shape, F32)
    for slot in range(SLOTS):
        top, part = stats(slot)
        ratio = jnp.exp2((top - highest) * EXP2_SCALE)
        if slot:
            ratio = jnp.where(live[slot], ratio, 0.0)
        total = total + ratio * part
        ratios.append(ratio)
    inverse = 1.0 / total
    deltas = delta_rows[0:4]
    for slot in range(SLOTS):
        factors = jnp.concatenate([ratios[slot] * inverse, deltas], axis=0)
        if slot == 0:
            fact_in[0] = factors
        else:
            fact_out[slot] = factors
            there = opposite(slot)
            remote(
                fact_out.at[slot], fact_in.at[there], fact_send.at[slot], fact_recv.at[there], at(DELTA[slot])
            ).start()

    for sign in (1, -1):
        wait_recv(gbuf, g_send, g_recv, slot_of(-16 * sign))
        relay_far(gbuf, g_send, g_recv, sign)

    def second_pass(slot, carry):
        @pl.when(jnp.logical_or(slot == 0, slot > 4))
        def _():
            @pl.when(slot > 0)
            def _():
                wait_recv(gbuf, g_send, g_recv, slot)

        @pl.when(slot > 0)
        def _():
            wait_recv(fact_in, fact_send, fact_recv, slot)

        for head in range(head_count):
            queries = spread(qbuf[slot, :, cols(head)])
            grads = spread(gbuf[slot, :, cols(head)])
            factor = fact_in[slot, pl.ds(head, 1), :]
            shift = fact_in[slot, pl.ds(4 + head, 1), :]
            prob_grad = dot_nt(vfull[head], grads)
            prob = ebuf[slot * head_count + head].astype(F32) * factor
            score_grad = (prob * (prob_grad - shift)).astype(BF16)
            dv_acc[head] += dot_nn(prob.astype(BF16), grads)
            dk_acc[head] += dot_nn(score_grad, queries)
            part_out[slot, pl.ds(head * HDIM, HDIM), :] = dot_nn(ktrans[head], score_grad).astype(BF16)

        @pl.when(slot > 0)
        def _():
            there = opposite(slot)
            remote(
                part_out.at[slot],
                part_in.at[there],
                part_send.at[slot],
                part_recv.at[there],
                at(slot_delta(slot)),
            ).start()

        return carry

    lax.fori_loop(0, SLOTS, second_pass, 0)

    def folded(wide_sum):
        both = wide_sum + pltpu.roll(wide_sum, HDIM, 1)
        return jnp.where(low, both[:pairs], both[pairs:])

    for head in range(head_count):
        dk_ref[:, cols(head)] = (folded(dk_acc[head]) * SCALING).astype(BF16)
        dv_ref[:, cols(head)] = folded(dv_acc[head]).astype(BF16)

    dq_acc[...] = part_out[0].astype(F32)

    def gather_part(slot, carry):
        wait_recv(part_in, part_send, part_recv, slot)
        dq_acc[...] += part_in[slot].astype(F32)
        return carry

    lax.fori_loop(1, SLOTS, gather_part, 0)
    for head in range(head_count):
        rows = dq_acc[pl.ds(head * HDIM, HDIM), :] * SCALING
        turned = jnp.transpose(jnp.concatenate([rows, rows], axis=0))
        dq_ref[:, cols(head)] = jnp.where(low, turned[:pairs], turned[pairs:]).astype(BF16)

    for step in range(1, heads):
        remote(
            ogbuf.at[my_head], ogbuf.at[my_head], og_send.at[step], og_recv.at[my_head], me, head_at(step)
        ).wait_send()

    def drain(slot, carry):
        wait_send(qbuf, q_send, q_recv, slot)
        wait_send(gbuf, g_send, g_recv, slot)
        wait_send(stat_in, stat_send, stat_recv, slot)
        wait_send(fact_in, fact_send, fact_recv, slot)
        wait_send(part_in, part_send, part_recv, slot)
        return carry

    lax.fori_loop(1, SLOTS, drain, 0)


def solution(mesh):
    blocks, heads = mesh.shape["seq"], mesh.shape["head"]

    def step(query_rows, key_rows, value_rows, attention_out, output_grad, out_weight, reach_mask):
        pairs, width = query_rows.shape
        head_count = width // (2 * HDIM)
        tokens = 2 * pairs
        vmem = pl.BlockSpec(memory_space=pltpu.VMEM)
        block = jax.ShapeDtypeStruct((pairs, width), BF16)
        dma = pltpu.SemaphoreType.DMA

        def body(*refs):
            kernel(blocks, heads, *refs)

        return pl.pallas_call(
            body,
            out_shape=(block, block, block),
            in_specs=[vmem] * 6 + [pl.BlockSpec(memory_space=pltpu.SMEM)],
            out_specs=(vmem, vmem, vmem),
            scratch_shapes=[
                pltpu.VMEM((SLOTS, pairs, width), BF16),
                pltpu.VMEM((SLOTS, pairs, width), BF16),
                pltpu.VMEM((heads, pairs, width), BF16),
                pltpu.VMEM((2, width, out_weight.shape[1]), BF16),
                pltpu.VMEM((SLOTS * head_count, tokens, tokens), BF16),
                pltpu.VMEM((head_count, tokens, 2 * HDIM), BF16),
                pltpu.VMEM((head_count, tokens, 2 * HDIM), BF16),
                pltpu.VMEM((head_count, HDIM, tokens), BF16),
                pltpu.VMEM((8, tokens), F32),
                pltpu.VMEM((SLOTS, 8, tokens), F32),
                pltpu.VMEM((SLOTS, 8, tokens), F32),
                pltpu.VMEM((SLOTS, 8, tokens), F32),
                pltpu.VMEM((SLOTS, 8, tokens), F32),
                pltpu.VMEM((SLOTS, head_count * HDIM, tokens), BF16),
                pltpu.VMEM((SLOTS, head_count * HDIM, tokens), BF16),
                pltpu.VMEM((head_count, tokens, 2 * HDIM), F32),
                pltpu.VMEM((head_count, tokens, 2 * HDIM), F32),
                pltpu.VMEM((head_count * HDIM, tokens), F32),
                dma((SLOTS,)),
                dma((SLOTS,)),
                dma((SLOTS,)),
                dma((SLOTS,)),
                dma((heads,)),
                dma((heads,)),
                dma((SLOTS,)),
                dma((SLOTS,)),
                dma((SLOTS,)),
                dma((SLOTS,)),
                dma((SLOTS,)),
                dma((SLOTS,)),
            ],
            compiler_params=pltpu.CompilerParams(
                collective_id=0, has_side_effects=True, vmem_limit_bytes=52 * 1024 * 1024
            ),
            cost_estimate=pl.CostEstimate(flops=8 * 10**9, bytes_accessed=2 * 10**6, transcendentals=6 * 10**6),
        )(query_rows, key_rows, value_rows, attention_out, output_grad, out_weight, reach_mask)

    rows = P("seq", "head")
    return jax.shard_map(
        step,
        mesh=mesh,
        in_specs=(rows, rows, rows, rows, rows, P("head", None), P("seq", None)),
        out_specs=(rows, rows, rows),
        check_vma=False,
    )
```

profile of v0, /device:TPU:22, one launch (start us, length us, event | category | flops | bytes accessed | tf_op | source)
XLA Modules:
  0.0 95.7 jit_solution(9609730936205302823)
XLA Ops:
  0.6 0.0 copy-start
  0.6 1.0 copy-done
  1.6 0.0 copy-start.1
  1.6 0.9 copy-done.1
  2.5 0.0 copy-start.2
  2.5 0.9 copy-done.2
  3.4 0.0 copy-start.3
  3.4 0.9 copy-done.3
  4.3 0.0 copy-start.4
  4.3 0.9 copy-done.4
  5.2 0.0 copy-start.5
  5.2 0.9 copy-done.5
  6.1 0.0 copy-start.6
  6.2 0.7 copy-done.6
  6.8 86.9 %shard_map.94 = (bf16[192,384]{1,0:T(8,128)(2,1)S(1)}, bf16[192,384]{1,0:T(8,128)(2,1)S(1)}, bf16[192,384]{1,0:T(8,128)(2,1)S(1)}) custom-call(bf16[192,384]{1,0:T(8,128)(2,1)S(1)} %copy-done.1, bf16[192,384]{1,0:T(8,128)(2,1)S(1)} %copy-done.2, bf16[192,384]{1,0:T(8,128)(2,1)S(1)} %copy-done.3, bf16[192,384]{1,0:T(8,128)(2,1)S(1)} %copy-done.4, ...), custom_call_target="tpu_custom_call" | custom-call | flops 8000000000 | bytes 2000000 | tf_op jit(solution)/shard_map/pallas_call | solution.py:400
  93.8 0.7 copy.13
  94.4 0.7 copy.14
  95.1 0.7 copy.15
Async XLA Ops:
  0.6 1.0 %copy-start = (bf16[192,768]{1,0:T(8,128)(2,1)S(1)}, bf16[192,768]{1,0:T(8,128)(2,1)}, u32[]{:S(2)}) copy-start(bf16[192,768]{1,0:T(8,128)(2,1)} %refs_5_.1) | copy-start | bytes 884740
  1.6 0.9 copy-start.1
  2.5 0.9 copy-start.2
  3.4 0.9 copy-start.3
  4.3 0.9 copy-start.4
  5.2 0.9 copy-start.5
  6.1 0.7 copy-start.6
where the time goes:
time: 96 us; the launch traced here: 95.7 us
  Pallas kernels  86.9 us (91%)
  local copies, waits for them, and re-layouts  8.14 us (8%)
    pallas_call x1, Pallas kernels, step(): pl.pallas_call(body, out_shape=(block, block, block), in_specs=[vmem] * 6...  86.9 us
    unnamed x17, local copies, waits for them, and re-layouts  8.14 us

commit v1 on v0

v1 whole, which is shorter than its diff:
```python
import jax
import jax.numpy as jnp
from jax import lax
from jax.experimental import pallas as pl
from jax.experimental.pallas import tpu as pltpu
from jax.sharding import PartitionSpec as P

MESH = pl.DeviceIdType.MESH
HDIM = 64
PLANE = 8
SLOTS = 13
DELTA = (0, -8, 8, -16, 16, -1, 1, -2, 2, -4, 4, -32, 32)
SCALING = HDIM**-0.5
EXP2_SCALE = SCALING * 1.4426950408889634
F32 = jnp.float32
BF16 = jnp.bfloat16


def mask_column(delta):
    return 2 * (abs(delta).bit_length() - 1) + (delta < 0)


def opposite(slot):
    return slot + 1 - 2 * ((slot + 1) % 2)


def slot_delta(slot):
    pair = (slot + 1) // 2
    power = (pair + 2) % 5 + 2 * (pair // 6)
    size = (1 + power % 2) * (1 + 3 * ((power // 2) % 2)) * (1 + 15 * (power // 4))
    return size * (1 - 2 * (slot % 2))


def dot_nt(left, right):
    return lax.dot_general(left, right, (((1,), (1,)), ((), ())), preferred_element_type=F32)


def dot_nn(left, right):
    return jnp.dot(left, right, preferred_element_type=F32)


TAIL = 16


def kernel(
    blocks,
    heads,
    q_hbm,
    k_hbm,
    v_hbm,
    ao_hbm,
    og_hbm,
    w_hbm,
    reach_hbm,
    dq_ref,
    dk_ref,
    dv_ref,
    k_ref,
    v_ref,
    ao_ref,
    w_ref,
    reach_ref,
    qbuf,
    gbuf,
    ogbuf,
    wide,
    ebuf,
    ubuf,
    kfull,
    vfull,
    ktrans,
    stat_out,
    stat_in,
    fact_out,
    fact_in,
    dq_raw,
    part_out,
    part_in,
    dk_acc,
    dv_acc,
    dq_acc,
    local_sem,
    q_send,
    q_recv,
    g_send,
    g_recv,
    og_send,
    og_recv,
    stat_send,
    stat_recv,
    fact_send,
    fact_recv,
    part_send,
    part_recv,
):
    _, pairs, width = qbuf.shape
    head_count = width // (2 * HDIM)
    me = lax.axis_index("seq")
    my_head = lax.axis_index("head")
    spot = lax.rem(me, PLANE)
    plane_start = me - spot

    def at(delta):
        return lax.rem(me + delta + blocks, blocks)

    def in_plane(delta):
        return plane_start + lax.rem(spot + delta + PLANE, PLANE)

    def stays(delta):
        return spot + delta < PLANE if delta > 0 else spot + delta >= 0

    def head_at(step):
        return lax.rem(my_head + step, heads)

    barrier = pltpu.get_barrier_semaphore()
    for delta in DELTA[1:]:
        pl.semaphore_signal(barrier, inc=1, device_id=(at(delta), my_head), device_id_type=MESH)
    for delta in (-1, 1, -2, 2, 4):
        pl.semaphore_signal(barrier, inc=1, device_id=(in_plane(delta), my_head), device_id_type=MESH)
    for step in range(1, heads):
        pl.semaphore_signal(barrier, inc=1, device_id=(me, head_at(step)), device_id_type=MESH)

    loads = [
        pltpu.make_async_copy(src, dst, local_sem.at[i])
        for i, (src, dst) in enumerate(
            [
                (k_hbm, k_ref),
                (q_hbm, qbuf.at[0]),
                (v_hbm, v_ref),
                (w_hbm, w_ref),
                (ao_hbm, ao_ref),
                (og_hbm, ogbuf.at[my_head]),
                (reach_hbm, reach_ref),
            ]
        )
    ]
    for load in loads:
        load.start()

    lane = lax.broadcasted_iota(jnp.int32, (1, 2 * HDIM), 1)
    low = lane < HDIM
    low_f = low.astype(F32)
    low_b = low_f.astype(BF16)
    high_b = (1.0 - low_f).astype(BF16)

    def cols(head):
        return pl.ds(head * 2 * HDIM, 2 * HDIM)

    def head_rows(head):
        return pl.ds(head * HDIM, HDIM)

    def doubled(tile):
        tile = tile.astype(F32)
        turned = pltpu.roll(tile, HDIM, 1)
        return jnp.concatenate([jnp.where(low, tile, turned), jnp.where(low, turned, tile)], axis=0)

    def spread(tile):
        return jnp.concatenate([tile * low_b, tile * high_b], axis=0)

    pl.semaphore_wait(barrier, 17 + heads - 1)

    def remote(src, dst, send_sem, recv_sem, seq, head=None):
        return pltpu.make_async_remote_copy(
            src_ref=src,
            dst_ref=dst,
            send_sem=send_sem,
            recv_sem=recv_sem,
            device_id=(seq, my_head if head is None else head),
            device_id_type=MESH,
        )

    queries_net = (qbuf, q_send, q_recv)
    grads_net = (gbuf, g_send, g_recv)
    stats_net = (stat_in, stat_send, stat_recv)
    facts_net = (fact_in, fact_send, fact_recv)
    parts_net = (part_in, part_send, part_recv)

    def move(net, src, dst_slot, seq):
        buf, send, recv = net
        return remote(src, buf.at[dst_slot], send.at[dst_slot], recv.at[dst_slot], seq)

    def wait_recv(net, slot):
        move(net, net[0].at[slot], slot, at(8)).wait_recv()

    def wait_send(net, slot):
        move(net, net[0].at[slot], slot, at(8)).wait_send()

    def slot_of(delta):
        return DELTA.index(delta)

    def send_own(net, src):
        for sign in (1, -1):
            move(net, src, slot_of(-8 * sign), at(8 * sign)).start()

    def send_plane_own(net, src):
        for delta in (4, -4, 2, -2, 1, -1):

            @pl.when(stays(delta))
            def _():
                move(net, src, slot_of(-delta), in_plane(delta)).start()

    def relay_near(net, sign):
        source = net[0].at[slot_of(-8 * sign)]
        move(net, source, slot_of(-16 * sign), at(8 * sign)).start()
        for size in (4, 2, 1):
            delta = size * sign

            @pl.when(jnp.logical_not(stays(delta)))
            def _():
                move(net, source, slot_of(-delta), in_plane(delta)).start()

    def relay_far(net, sign):
        move(net, net[0].at[slot_of(-16 * sign)], slot_of(-32 * sign), at(16 * sign)).start()

    send_own(queries_net, q_hbm)
    for step in range(1, heads):
        remote(og_hbm, ogbuf.at[my_head], og_send.at[step], og_recv.at[my_head], me, head_at(step)).start()
    send_plane_own(queries_net, q_hbm)

    for load in loads:
        load.wait()
    for head in range(head_count):
        keys = doubled(k_ref[:, cols(head)])
        kfull[head] = keys.astype(BF16)
        ktrans[head] = jnp.transpose(keys)[:HDIM].astype(BF16)
        vfull[head] = doubled(v_ref[:, cols(head)]).astype(BF16)
        dk_acc[head] = jnp.zeros((2 * pairs, 2 * HDIM), F32)
        dv_acc[head] = jnp.zeros((2 * pairs, 2 * HDIM), F32)
    wide[...] = jnp.zeros(wide.shape, BF16)
    for head in range(head_count):
        rows = w_ref[pl.ds(head * HDIM, HDIM), :]
        for parity in range(2):
            wide[parity, pl.ds((head * 2 + parity) * HDIM, HDIM), :] = rows

    def grads_of_attention():
        for step in range(1, heads):
            other = head_at(step)
            remote(og_hbm, ogbuf.at[other], og_send.at[step], og_recv.at[other], me, other).wait_recv()
        total = jnp.zeros((pairs, width), F32)
        for chunk in range(heads):
            half = chunk % 2
            total = total + dot_nt(ogbuf[chunk], wide[chunk // 2, :, pl.ds(half * width, width)])
        grads = total.astype(BF16)
        gbuf[0, :pairs, :] = grads
        product = grads.astype(F32) * ao_ref[...].astype(F32)
        column = lax.broadcasted_iota(jnp.int32, (1, width), 1)
        first = lax.rem(column, 2 * HDIM) < HDIM
        both = jnp.concatenate([jnp.where(first, product, 0.0), jnp.where(first, 0.0, product)], axis=0)
        top = both.astype(BF16)
        rest = (both - top.astype(F32)).astype(BF16)
        chooser = (
            lax.broadcasted_iota(jnp.int32, (8, width), 1) // (2 * HDIM)
            == lax.broadcasted_iota(jnp.int32, (8, width), 0)
        )
        chooser = chooser.astype(F32).astype(BF16)
        delta = dot_nt(chooser, top) + dot_nt(chooser, rest)
        delta_top = delta.astype(BF16)
        delta_rest = (delta - delta_top.astype(F32)).astype(BF16)
        gbuf[0, pairs:, :] = jnp.concatenate([delta_top, delta_rest], axis=0)

    def first_pass(slot, carry):
        @pl.when(slot > 0)
        def _():
            wait_recv(queries_net, slot)

        for sign in (1, -1):

            @pl.when(slot == slot_of(-8 * sign))
            def _():
                relay_near(queries_net, sign)

            @pl.when(slot == slot_of(-16 * sign))
            def _():
                relay_far(queries_net, sign)

        @pl.when(slot == 5)
        def _():
            grads_of_attention()
            send_own(grads_net, gbuf.at[0])
            send_plane_own(grads_net, gbuf.at[0])

        tops, sums = [], []
        for head in range(head_count):
            queries = spread(qbuf[slot, :, cols(head)])
            scores = dot_nt(kfull[head], queries)
            top = jnp.max(scores, axis=0, keepdims=True)
            weights = jnp.exp2((scores - top) * EXP2_SCALE)
            tops.append(top)
            sums.append(jnp.sum(weights, axis=0, keepdims=True))
            ebuf[slot * head_count + head] = weights.astype(BF16)
        stat_out[slot] = jnp.concatenate(tops + tops[:1] + sums + sums[:1], axis=0)

        @pl.when(slot > 0)
        def _():
            there = opposite(slot)
            remote(
                stat_out.at[slot], stat_in.at[there], stat_send.at[slot], stat_recv.at[there], at(slot_delta(slot))
            ).start()

        return carry

    lax.fori_loop(0, SLOTS, first_pass, 0)

    for sign in (1, -1):
        wait_recv(grads_net, slot_of(-8 * sign))
        relay_near(grads_net, sign)

    def share_factors():
        live = [None] + [reach_ref[0, mask_column(delta)] > 0 for delta in DELTA[1:]]
        for slot in range(1, SLOTS):
            wait_recv(stats_net, slot)

        def stats(slot):
            both = stat_out[0] if slot == 0 else stat_in[slot]
            return both[0:4], both[4:8]

        highest = stats(0)[0]
        for slot in range(1, SLOTS):
            highest = jnp.maximum(highest, jnp.where(live[slot], stats(slot)[0], -1e30))
        ratios = []
        total = jnp.zeros(highest.shape, F32)
        for slot in range(SLOTS):
            top, part = stats(slot)
            if slot:
                top = jnp.where(live[slot], top, -1e30)
            ratio = jnp.exp2((top - highest) * EXP2_SCALE)
            if slot:
                ratio = jnp.where(live[slot], ratio, 0.0)
            total = total + ratio * part
            ratios.append(ratio)
        inverse = 1.0 / total
        for slot in range(SLOTS):
            factors = ratios[slot] * inverse
            factors = jnp.concatenate([factors, factors], axis=0)
            if slot == 0:
                fact_in[0] = factors
            else:
                fact_out[slot] = factors
                there = opposite(slot)
                remote(
                    fact_out.at[slot], fact_in.at[there], fact_send.at[slot], fact_recv.at[there], at(DELTA[slot])
                ).start()

    def scaled(slot):
        factors = fact_in[slot]
        return jnp.concatenate(
            [dq_raw[slot, head_rows(head), :] * factors[head : head + 1] for head in range(head_count)], axis=0
        )

    def return_part(slot, seq):
        part_out[slot] = scaled(slot).astype(BF16)
        move(parts_net, part_out.at[slot], slot, seq).start()

    def second_pass(slot, carry):
        @pl.when(slot == 3)
        def _():
            for sign in (1, -1):
                wait_recv(grads_net, slot_of(-16 * sign))
                relay_far(grads_net, sign)
            share_factors()

        @pl.when(slot == 11)
        def _():
            for delta in (4, -4, 2, -2, 1, -1):
                wait_recv(facts_net, slot_of(delta))
                return_part(slot_of(delta), in_plane(delta))

        @pl.when(slot > 4)
        def _():
            wait_recv(grads_net, slot)

        tail = gbuf[slot, pairs:, :].astype(F32)
        for head in range(head_count):
            grads = spread(gbuf[slot, :pairs, cols(head)])
            shift = tail[head : head + 1] + tail[8 + head : 9 + head]
            prob_grad = dot_nt(vfull[head], grads)
            weights = ebuf[slot * head_count + head].astype(F32)
            raw = (weights * (prob_grad - shift)).astype(BF16)
            ubuf[slot * head_count + head] = raw
            dq_raw[slot, head_rows(head), :] = dot_nn(ktrans[head], raw)
        return carry

    lax.fori_loop(0, SLOTS, second_pass, 0)

    for sign in (1, -1):
        slot = slot_of(-32 * sign)
        wait_recv(facts_net, slot)
        return_part(slot, at(-16 * sign))
    for slot in (1, 2, 3, 4):
        wait_recv(facts_net, slot)
    for slot in (0, 1, 2):
        dq_acc[slot] = scaled(slot)

    def third_pass(slot, carry):
        factors = fact_in[slot]
        for head in range(head_count):
            factor = factors[head : head + 1]
            queries = spread(qbuf[slot, :, cols(head)])
            grads = spread(gbuf[slot, :pairs, cols(head)])
            prob = (ebuf[slot * head_count + head].astype(F32) * factor).astype(BF16)
            score_grad = (ubuf[slot * head_count + head].astype(F32) * factor).astype(BF16)
            dv_acc[head] += dot_nn(prob, grads)
            dk_acc[head] += dot_nn(score_grad, queries)
        return carry

    lax.fori_loop(0, SLOTS, third_pass, 0)

    for sign in (1, -1):
        far, near = slot_of(-32 * sign), slot_of(-16 * sign)
        wait_recv(parts_net, far)
        part_out[near] = (scaled(near) + part_in[far].astype(F32)).astype(BF16)
        move(parts_net, part_out.at[near], near, at(-8 * sign)).start()

    for delta in (4, -4, 2, -2, 1, -1):
        slot = slot_of(-delta)
        owner = jnp.where(stays(delta), 0, slot_of(-8) if delta > 0 else slot_of(8))
        wait_recv(parts_net, slot)
        dq_acc[owner] += part_in[slot].astype(F32)

    def folded(wide_sum):
        both = wide_sum + pltpu.roll(wide_sum, HDIM, 1)
        return jnp.where(low, both[:pairs], both[pairs:])

    for head in range(head_count):
        dk_ref[:, cols(head)] = (folded(dk_acc[head]) * SCALING).astype(BF16)
        dv_ref[:, cols(head)] = folded(dv_acc[head]).astype(BF16)

    for sign in (1, -1):
        near, next_to = slot_of(-16 * sign), slot_of(-8 * sign)
        wait_recv(parts_net, near)
        part_out[next_to] = (dq_acc[next_to] + part_in[near].astype(F32)).astype(BF16)
        move(parts_net, part_out.at[next_to], next_to, at(-8 * sign)).start()

    for sign in (1, -1):
        slot = slot_of(-8 * sign)
        wait_recv(parts_net, slot)
    total = (dq_acc[0] + part_in[1].astype(F32) + part_in[2].astype(F32)) * SCALING
    for head in range(head_count):
        rows = total[head * HDIM : (head + 1) * HDIM]
        turned = jnp.transpose(jnp.concatenate([rows, rows], axis=0))
        dq_ref[:, cols(head)] = jnp.where(low, turned[:pairs], turned[pairs:]).astype(BF16)

    for step in range(1, heads):
        remote(og_hbm, ogbuf.at[my_head], og_send.at[step], og_recv.at[my_head], me, head_at(step)).wait_send()

    def drain(slot, carry):
        for net in (queries_net, grads_net, stats_net, facts_net, parts_net):
            wait_send(net, slot)
        return carry

    lax.fori_loop(1, SLOTS, drain, 0)


def solution(mesh):
    blocks, heads = mesh.shape["seq"], mesh.shape["head"]

    def step(query_rows, key_rows, value_rows, attention_out, output_grad, out_weight, reach_mask):
        pairs, width = query_rows.shape
        head_count = width // (2 * HDIM)
        tokens = 2 * pairs
        vmem = pl.BlockSpec(memory_space=pltpu.VMEM)
        block = jax.ShapeDtypeStruct((pairs, width), BF16)
        dma = pltpu.SemaphoreType.DMA

        def body(*refs):
            kernel(blocks, heads, *refs)

        return pl.pallas_call(
            body,
            out_shape=(block, block, block),
            in_specs=[pl.BlockSpec(memory_space=pltpu.HBM)] * 7,
            out_specs=(vmem, vmem, vmem),
            scratch_shapes=[
                pltpu.VMEM((pairs, width), BF16),
                pltpu.VMEM((pairs, width), BF16),
                pltpu.VMEM((pairs, width), BF16),
                pltpu.VMEM(out_weight.shape, BF16),
                pltpu.SMEM(reach_mask.shape, jnp.int32),
                pltpu.VMEM((SLOTS, pairs, width), BF16),
                pltpu.VMEM((SLOTS, pairs + TAIL, width), BF16),
                pltpu.VMEM((heads, pairs, width), BF16),
                pltpu.VMEM((2, width, out_weight.shape[1]), BF16),
                pltpu.VMEM((SLOTS * head_count, tokens, tokens), BF16),
                pltpu.VMEM((SLOTS * head_count, tokens, tokens), BF16),
                pltpu.VMEM((head_count, tokens, 2 * HDIM), BF16),
                pltpu.VMEM((head_count, tokens, 2 * HDIM), BF16),
                pltpu.VMEM((head_count, HDIM, tokens), BF16),
                pltpu.VMEM((SLOTS, 8, tokens), F32),
                pltpu.VMEM((SLOTS, 8, tokens), F32),
                pltpu.VMEM((SLOTS, 8, tokens), F32),
                pltpu.VMEM((SLOTS, 8, tokens), F32),
                pltpu.VMEM((SLOTS, head_count * HDIM, tokens), F32),
                pltpu.VMEM((SLOTS, head_count * HDIM, tokens), BF16),
                pltpu.VMEM((SLOTS, head_count * HDIM, tokens), BF16),
                pltpu.VMEM((head_count, tokens, 2 * HDIM), F32),
                pltpu.VMEM((head_count, tokens, 2 * HDIM), F32),
                pltpu.VMEM((3, head_count * HDIM, tokens), F32),
                dma((7,)),
                dma((SLOTS,)),
                dma((SLOTS,)),
                dma((SLOTS,)),
                dma((SLOTS,)),
                dma((heads,)),
                dma((heads,)),
                dma((SLOTS,)),
                dma((SLOTS,)),
                dma((SLOTS,)),
                dma((SLOTS,)),
                dma((SLOTS,)),
                dma((SLOTS,)),
            ],
            compiler_params=pltpu.CompilerParams(
                collective_id=0, has_side_effects=True, vmem_limit_bytes=56 * 1024 * 1024
            ),
            cost_estimate=pl.CostEstimate(flops=8 * 10**9, bytes_accessed=2 * 10**6, transcendentals=6 * 10**6),
        )(query_rows, key_rows, value_rows, attention_out, output_grad, out_weight, reach_mask)

    rows = P("seq", "head")
    return jax.shard_map(
        step,
        mesh=mesh,
        in_specs=(rows, rows, rows, rows, rows, P("head", None), P("seq", None)),
        out_specs=(rows, rows, rows),
        check_vma=False,
    )
```

time: 96 us -> 86.2 us (0.90)
  the two profiles are of different devices: /device:TPU:22 before, /device:TPU:8 now
where the time goes in v1:
time: 86.2 us; the launch traced here: 86.1 us
  Pallas kernels  82.2 us (95%)
  local copies, waits for them, and re-layouts  3.25 us (4%)
    pallas_call x1, Pallas kernels, step(): pl.pallas_call(body, out_shape=(block, block, block), in_specs=[pl.BlockS...  82.2 us
    unnamed x7, local copies, waits for them, and re-layouts  3.25 us

profile of v1, /device:TPU:8, one launch (start us, length us, event | category | flops | bytes accessed | tf_op | source)
XLA Modules:
  0.0 86.1 jit_solution(3413922881776744576)
XLA Ops:
  0.6 82.2 %shard_map.94 = (bf16[192,384]{1,0:T(8,128)(2,1)}, bf16[192,384]{1,0:T(8,128)(2,1)}, bf16[192,384]{1,0:T(8,128)(2,1)}) custom-call(bf16[192,384]{1,0:T(8,128)(2,1)} %refs_0_.1, bf16[192,384]{1,0:T(8,128)(2,1)} %refs_1_.1, bf16[192,384]{1,0:T(8,128)(2,1)} %refs_2_.1, bf16[192,384]{1,0:T(8,128)(2,1)} %refs_3_.1, bf16[192,384]{1,0:T(8,128)(2,1)} %refs_4_.1, ...), custom_call_target="tpu_custom_call" | custom-call | flops 8000000000 | bytes 2000000 | tf_op jit(solution)/shard_map/pallas_call | solution.py:468
  82.8 0.0 copy-start.1
  82.8 1.6 %copy.13 = bf16[192,384]{1,0:T(8,128)(2,1)} copy(bf16[192,384]{1,0:T(8,128)(2,1)} %get-tuple-element.6) | data formatting | bytes 294912
  84.5 0.0 copy-done.1
  84.5 0.0 copy-start
  84.5 0.7 copy.14
  85.1 0.3 copy-done
  85.4 0.7 copy.15
Async XLA Ops:
  82.8 1.6 %copy-start.1 = (bf16[192,384]{1,0:T(8,128)(2,1)S(1)}, bf16[192,384]{1,0:T(8,128)(2,1)}, u32[]{:S(2)}) copy-start(bf16[192,384]{1,0:T(8,128)(2,1)} %get-tuple-element.7) | copy-start | bytes 442372
  84.5 1.0 %copy-start = (bf16[192,384]{1,0:T(8,128)(2,1)S(1)}, bf16[192,384]{1,0:T(8,128)(2,1)}, u32[]{:S(2)}) copy-start(bf16[192,384]{1,0:T(8,128)(2,1)} %get-tuple-element.8) | copy-start | bytes 442372

commit v2 on v1

--- a/solution.py
+++ b/solution.py
@@ -31,6 +31,19 @@
     return size * (1 - 2 * (slot % 2))
 
 
+def slot_column(slot):
+    pair = (slot + 1) // 2
+    power = (pair + 2) % 5 + 2 * (pair // 6)
+    return 2 * power + 1 - slot % 2
+
+
+def turn_slot(turn, spot):
+    place = turn - 5
+    sign = lax.rem(place // 3 + 1 - spot // (PLANE // 2), 2)
+    inner = 5 + 2 * lax.rem(place, 3) + sign
+    return jnp.where(jnp.logical_and(turn >= 5, turn <= 10), inner, turn)
+
+
 def dot_nt(left, right):
     return lax.dot_general(left, right, (((1,), (1,)), ((), ())), preferred_element_type=F32)
 
@@ -40,6 +53,7 @@
 
 
 TAIL = 16
+DEAD = -1e30
 
 
 def kernel(
@@ -76,9 +90,10 @@
     dq_raw,
     part_out,
     part_in,
+    row_top,
+    norm,
     dk_acc,
     dv_acc,
-    dq_acc,
     local_sem,
     q_send,
     q_recv,
@@ -95,6 +110,7 @@
 ):
     _, pairs, width = qbuf.shape
     head_count = width // (2 * HDIM)
+    width_rows = head_count * HDIM
     me = lax.axis_index("seq")
     my_head = lax.axis_index("head")
     spot = lax.rem(me, PLANE)
@@ -256,9 +272,16 @@
         delta = dot_nt(chooser, top) + dot_nt(chooser, rest)
         delta_top = delta.astype(BF16)
         delta_rest = (delta - delta_top.astype(F32)).astype(BF16)
-        gbuf[0, pairs:, :] = jnp.concatenate([delta_top, delta_rest], axis=0)
-
-    def first_pass(slot, carry):
+        wide_lane = lax.broadcasted_iota(jnp.int32, (1, width), 1)
+        reach = jnp.zeros((1, width), F32)
+        for entry in range(reach_ref.shape[1]):
+            reach = jnp.where(wide_lane == entry, (reach_ref[0, entry] > 0).astype(F32), reach)
+        reach = reach.astype(BF16)
+        gbuf[0, pairs:, :] = jnp.concatenate([delta_top[:4], reach, delta_top[5:], delta_rest], axis=0)
+
+    def first_pass(turn, carry):
+        slot = turn_slot(turn, spot)
+
         @pl.when(slot > 0)
         def _():
             wait_recv(queries_net, slot)
@@ -273,11 +296,17 @@
             def _():
                 relay_far(queries_net, sign)
 
-        @pl.when(slot == 5)
+        @pl.when(turn == 5)
         def _():
             grads_of_attention()
             send_own(grads_net, gbuf.at[0])
             send_plane_own(grads_net, gbuf.at[0])
+
+        @pl.when(slot == 11)
+        def _():
+            for sign in (1, -1):
+                wait_recv(grads_net, slot_of(-8 * sign))
+                relay_near(grads_net, sign)
 
         tops, sums = [], []
         for head in range(head_count):
@@ -301,10 +330,6 @@
 
     lax.fori_loop(0, SLOTS, first_pass, 0)
 
-    for sign in (1, -1):
-        wait_recv(grads_net, slot_of(-8 * sign))
-        relay_near(grads_net, sign)
-
     def share_factors():
         live = [None] + [reach_ref[0, mask_column(delta)] > 0 for delta in DELTA[1:]]
         for slot in range(1, SLOTS):
@@ -316,19 +341,20 @@
 
         highest = stats(0)[0]
         for slot in range(1, SLOTS):
-            highest = jnp.maximum(highest, jnp.where(live[slot], stats(slot)[0], -1e30))
+            highest = jnp.maximum(highest, jnp.where(live[slot], stats(slot)[0], DEAD))
         ratios = []
         total = jnp.zeros(highest.shape, F32)
         for slot in range(SLOTS):
             top, part = stats(slot)
             if slot:
-                top = jnp.where(live[slot], top, -1e30)
+                top = jnp.where(live[slot], top, DEAD)
             ratio = jnp.exp2((top - highest) * EXP2_SCALE)
             if slot:
                 ratio = jnp.where(live[slot], ratio, 0.0)
             total = total + ratio * part
             ratios.append(ratio)
         inverse = 1.0 / total
+        norm[...] = jnp.concatenate([highest, inverse], axis=0)
         for slot in range(SLOTS):
             factors = ratios[slot] * inverse
             factors = jnp.concatenate([factors, factors], axis=0)
@@ -341,17 +367,33 @@
                     fact_out.at[slot], fact_in.at[there], fact_send.at[slot], fact_recv.at[there], at(DELTA[slot])
                 ).start()
 
-    def scaled(slot):
-        factors = fact_in[slot]
-        return jnp.concatenate(
-            [dq_raw[slot, head_rows(head), :] * factors[head : head + 1] for head in range(head_count)], axis=0
-        )
-
     def return_part(slot, seq):
-        part_out[slot] = scaled(slot).astype(BF16)
+        tops = row_top[slot]
+        first = tops.astype(BF16)
+        tops = tops - first.astype(F32)
+        second = tops.astype(BF16)
+        third = (tops - second.astype(F32)).astype(BF16)
+        part_out[slot, :width_rows, :] = dq_raw[slot].astype(BF16)
+        part_out[slot, width_rows:, :] = jnp.concatenate([first, second, third, third], axis=0)
         move(parts_net, part_out.at[slot], slot, seq).start()
 
-    def second_pass(slot, carry):
+    def merge(target, slot):
+        wait_recv(parts_net, slot)
+        tail = part_in[slot, width_rows:, :].astype(F32)
+        theirs = tail[0:4] + tail[4:8] + tail[8:12]
+        ours = row_top[target]
+        top = jnp.maximum(ours, theirs)
+        ours = jnp.exp2((ours - top) * EXP2_SCALE)
+        theirs = jnp.exp2((theirs - top) * EXP2_SCALE)
+        row_top[target] = top
+        for head in range(head_count):
+            rows = head_rows(head)
+            one = slice(head, head + 1)
+            dq_raw[target, rows, :] = dq_raw[target, rows, :] * ours[one] + part_in[slot, rows, :].astype(F32) * theirs[one]
+
+    def second_pass(turn, carry):
+        slot = turn_slot(turn, spot)
+
         @pl.when(slot == 3)
         def _():
             for sign in (1, -1):
@@ -359,17 +401,15 @@
                 relay_far(grads_net, sign)
             share_factors()
 
-        @pl.when(slot == 11)
-        def _():
-            for delta in (4, -4, 2, -2, 1, -1):
-                wait_recv(facts_net, slot_of(delta))
-                return_part(slot_of(delta), in_plane(delta))
-
         @pl.when(slot > 4)
         def _():
             wait_recv(grads_net, slot)
 
         tail = gbuf[slot, pairs:, :].astype(F32)
+        column = slot_column(slot)
+        chosen = jnp.where(lax.broadcasted_iota(jnp.int32, (1, width), 1) == column, tail[4:5], 0.0)
+        alive = jnp.maximum(jnp.sum(chosen, axis=1, keepdims=True), (slot == 0).astype(F32))
+        row_top[slot] = jnp.where(alive > 0.5, stat_out[slot, 0:4, :], DEAD)
         for head in range(head_count):
             grads = spread(gbuf[slot, :pairs, cols(head)])
             shift = tail[head : head + 1] + tail[8 + head : 9 + head]
@@ -377,21 +417,34 @@
             weights = ebuf[slot * head_count + head].astype(F32)
             raw = (weights * (prob_grad - shift)).astype(BF16)
             ubuf[slot * head_count + head] = raw
-            dq_raw[slot, head_rows(head), :] = dot_nn(ktrans[head], raw)
+            dq_raw[slot, head_rows(head), :] = dot_nn(ktrans[head], raw) * alive
+
+        @pl.when(jnp.logical_and(slot > 4, slot < 11))
+        def _():
+            return_part(slot, in_plane(slot_delta(slot)))
+
+        @pl.when(slot == slot_of(-32))
+        def _():
+            return_part(slot_of(-32), at(-16))
+
+        @pl.when(slot == slot_of(32))
+        def _():
+            return_part(slot_of(32), at(16))
+
         return carry
 
     lax.fori_loop(0, SLOTS, second_pass, 0)
 
     for sign in (1, -1):
-        slot = slot_of(-32 * sign)
-        wait_recv(facts_net, slot)
-        return_part(slot, at(-16 * sign))
-    for slot in (1, 2, 3, 4):
-        wait_recv(facts_net, slot)
-    for slot in (0, 1, 2):
-        dq_acc[slot] = scaled(slot)
+        near = slot_of(-16 * sign)
+        merge(near, slot_of(-32 * sign))
+        return_part(near, at(-8 * sign))
 
     def third_pass(slot, carry):
+        @pl.when(slot > 0)
+        def _():
+            wait_recv(facts_net, slot)
+
         factors = fact_in[slot]
         for head in range(head_count):
             factor = factors[head : head + 1]
@@ -401,21 +454,20 @@
             score_grad = (ubuf[slot * head_count + head].astype(F32) * factor).astype(BF16)
             dv_acc[head] += dot_nn(prob, grads)
             dk_acc[head] += dot_nn(score_grad, queries)
+
+        @pl.when(slot == 6)
+        def _():
+            for delta in (2, -2, 4, -4, 1, -1):
+                owner = jnp.where(stays(delta), 0, slot_of(-8) if delta > 0 else slot_of(8))
+                merge(owner, slot_of(-delta))
+            for sign in (1, -1):
+                next_to = slot_of(-8 * sign)
+                merge(next_to, slot_of(-16 * sign))
+                return_part(next_to, at(-8 * sign))
+
         return carry
 
     lax.fori_loop(0, SLOTS, third_pass, 0)
-
-    for sign in (1, -1):
-        far, near = slot_of(-32 * sign), slot_of(-16 * sign)
-        wait_recv(parts_net, far)
-        part_out[near] = (scaled(near) + part_in[far].astype(F32)).astype(BF16)
-        move(parts_net, part_out.at[near], near, at(-8 * sign)).start()
-
-    for delta in (4, -4, 2, -2, 1, -1):
-        slot = slot_of(-delta)
-        owner = jnp.where(stays(delta), 0, slot_of(-8) if delta > 0 else slot_of(8))
-        wait_recv(parts_net, slot)
-        dq_acc[owner] += part_in[slot].astype(F32)
 
     def folded(wide_sum):
         both = wide_sum + pltpu.roll(wide_sum, HDIM, 1)
@@ -426,17 +478,10 @@
         dv_ref[:, cols(head)] = folded(dv_acc[head]).astype(BF16)
 
     for sign in (1, -1):
-        near, next_to = slot_of(-16 * sign), slot_of(-8 * sign)
-        wait_recv(parts_net, near)
-        part_out[next_to] = (dq_acc[next_to] + part_in[near].astype(F32)).astype(BF16)
-        move(parts_net, part_out.at[next_to], next_to, at(-8 * sign)).start()
-
-    for sign in (1, -1):
-        slot = slot_of(-8 * sign)
-        wait_recv(parts_net, slot)
-    total = (dq_acc[0] + part_in[1].astype(F32) + part_in[2].astype(F32)) * SCALING
+        merge(0, slot_of(-8 * sign))
+    final = jnp.exp2((row_top[0] - norm[0:4]) * EXP2_SCALE) * norm[4:8] * SCALING
     for head in range(head_count):
-        rows = total[head * HDIM : (head + 1) * HDIM]
+        rows = dq_raw[0, head_rows(head), :] * final[head : head + 1]
         turned = jnp.transpose(jnp.concatenate([rows, rows], axis=0))
         dq_ref[:, cols(head)] = jnp.where(low, turned[:pairs], turned[pairs:]).astype(BF16)
 
@@ -490,11 +535,12 @@
                 pltpu.VMEM((SLOTS, 8, tokens), F32),
                 pltpu.VMEM((SLOTS, 8, tokens), F32),
                 pltpu.VMEM((SLOTS, head_count * HDIM, tokens), F32),
-                pltpu.VMEM((SLOTS, head_count * HDIM, tokens), BF16),
-                pltpu.VMEM((SLOTS, head_count * HDIM, tokens), BF16),
+                pltpu.VMEM((SLOTS, head_count * HDIM + TAIL, tokens), BF16),
+                pltpu.VMEM((SLOTS, head_count * HDIM + TAIL, tokens), BF16),
+                pltpu.VMEM((SLOTS, 4, tokens), F32),
+                pltpu.VMEM((8, tokens), F32),
                 pltpu.VMEM((head_count, tokens, 2 * HDIM), F32),
                 pltpu.VMEM((head_count, tokens, 2 * HDIM), F32),
-                pltpu.VMEM((3, head_count * HDIM, tokens), F32),
                 dma((7,)),
                 dma((SLOTS,)),
                 dma((SLOTS,)),

time: 86.2 us -> 80.4 us (0.933)
  the two profiles are of different devices: /device:TPU:8 before, /device:TPU:32 now
where the time goes in v2:
time: 80.4 us; the launch traced here: 80.3 us
  Pallas kernels  76.4 us (95%)
  local copies, waits for them, and re-layouts  3.25 us (4%)
    pallas_call x1, Pallas kernels, step(): pl.pallas_call(body, out_shape=(block, block, block), in_specs=[pl.BlockS...  76.4 us
    unnamed x7, local copies, waits for them, and re-layouts  3.25 us

profile of v2, /device:TPU:32, one launch (start us, length us, event | category | flops | bytes accessed | tf_op | source)
XLA Modules:
  0.0 80.3 jit_solution(10137100184612482504)
XLA Ops:
  0.6 76.4 %shard_map.94 = (bf16[192,384]{1,0:T(8,128)(2,1)}, bf16[192,384]{1,0:T(8,128)(2,1)}, bf16[192,384]{1,0:T(8,128)(2,1)}) custom-call(bf16[192,384]{1,0:T(8,128)(2,1)} %refs_0_.1, bf16[192,384]{1,0:T(8,128)(2,1)} %refs_1_.1, bf16[192,384]{1,0:T(8,128)(2,1)} %refs_2_.1, bf16[192,384]{1,0:T(8,128)(2,1)} %refs_3_.1, bf16[192,384]{1,0:T(8,128)(2,1)} %refs_4_.1, ...), custom_call_target="tpu_custom_call" | custom-call | flops 8000000000 | bytes 2000000 | tf_op jit(solution)/shard_map/pallas_call | solution.py:513
  77.0 0.0 copy-start.1
  77.0 1.6 %copy.13 = bf16[192,384]{1,0:T(8,128)(2,1)} copy(bf16[192,384]{1,0:T(8,128)(2,1)} %get-tuple-element.6) | data formatting | bytes 294912
  78.6 0.0 copy-done.1
  78.7 0.0 copy-start
  78.7 0.7 copy.14
  79.3 0.3 copy-done
  79.6 0.7 copy.15
Async XLA Ops:
  77.0 1.6 %copy-start.1 = (bf16[192,384]{1,0:T(8,128)(2,1)S(1)}, bf16[192,384]{1,0:T(8,128)(2,1)}, u32[]{:S(2)}) copy-start(bf16[192,384]{1,0:T(8,128)(2,1)} %get-tuple-element.7) | copy-start | bytes 442372
  78.7 1.0 %copy-start = (bf16[192,384]{1,0:T(8,128)(2,1)S(1)}, bf16[192,384]{1,0:T(8,128)(2,1)}, u32[]{:S(2)}) copy-start(bf16[192,384]{1,0:T(8,128)(2,1)} %get-tuple-element.8) | copy-start | bytes 442372

commit v3 on v2

--- a/solution.py
+++ b/solution.py
@@ -458,8 +458,11 @@
         @pl.when(slot == 6)
         def _():
             for delta in (2, -2, 4, -4, 1, -1):
-                owner = jnp.where(stays(delta), 0, slot_of(-8) if delta > 0 else slot_of(8))
-                merge(owner, slot_of(-delta))
+
+                @pl.when(jnp.logical_not(stays(delta)))
+                def _():
+                    merge(slot_of(-8) if delta > 0 else slot_of(8), slot_of(-delta))
+
             for sign in (1, -1):
                 next_to = slot_of(-8 * sign)
                 merge(next_to, slot_of(-16 * sign))
@@ -476,6 +479,12 @@
     for head in range(head_count):
         dk_ref[:, cols(head)] = (folded(dk_acc[head]) * SCALING).astype(BF16)
         dv_ref[:, cols(head)] = folded(dv_acc[head]).astype(BF16)
+
+    for delta in (2, -2, 4, -4, 1, -1):
+
+        @pl.when(stays(delta))
+        def _():
+            merge(0, slot_of(-delta))
 
     for sign in (1, -1):
         merge(0, slot_of(-8 * sign))

time: 80.4 us -> 80.6 us (level)
  no operation moved by 1% of the time
where the time goes in v3:
time: 80.6 us; the launch traced here: 80.5 us
  Pallas kernels  76.6 us (95%)
  local copies, waits for them, and re-layouts  3.25 us (4%)
    pallas_call x1, Pallas kernels, step(): pl.pallas_call(body, out_shape=(block, block, block), in_specs=[pl.BlockS...  76.6 us
    unnamed x7, local copies, waits for them, and re-layouts  3.25 us

profile of v3, /device:TPU:32, one launch (start us, length us, event | category | flops | bytes accessed | tf_op | source)
XLA Modules:
  0.0 80.5 jit_solution(1887835934974668491)
XLA Ops:
  0.6 76.6 %shard_map.94 = (bf16[192,384]{1,0:T(8,128)(2,1)}, bf16[192,384]{1,0:T(8,128)(2,1)}, bf16[192,384]{1,0:T(8,128)(2,1)}) custom-call(bf16[192,384]{1,0:T(8,128)(2,1)} %refs_0_.1, bf16[192,384]{1,0:T(8,128)(2,1)} %refs_1_.1, bf16[192,384]{1,0:T(8,128)(2,1)} %refs_2_.1, bf16[192,384]{1,0:T(8,128)(2,1)} %refs_3_.1, bf16[192,384]{1,0:T(8,128)(2,1)} %refs_4_.1, ...), custom_call_target="tpu_custom_call" | custom-call | flops 8000000000 | bytes 2000000 | tf_op jit(solution)/shard_map/pallas_call | solution.py:522
  77.2 0.0 copy-start.1
  77.2 1.6 %copy.13 = bf16[192,384]{1,0:T(8,128)(2,1)} copy(bf16[192,384]{1,0:T(8,128)(2,1)} %get-tuple-element.6) | data formatting | bytes 294912
  78.8 0.0 copy-done.1
  78.8 0.0 copy-start
  78.8 0.7 copy.14
  79.5 0.3 copy-done
  79.8 0.7 copy.15
Async XLA Ops:
  77.2 1.6 %copy-start.1 = (bf16[192,384]{1,0:T(8,128)(2,1)S(1)}, bf16[192,384]{1,0:T(8,128)(2,1)}, u32[]{:S(2)}) copy-start(bf16[192,384]{1,0:T(8,128)(2,1)} %get-tuple-element.7) | copy-start | bytes 442372
  78.8 1.0 %copy-start = (bf16[192,384]{1,0:T(8,128)(2,1)S(1)}, bf16[192,384]{1,0:T(8,128)(2,1)}, u32[]{:S(2)}) copy-start(bf16[192,384]{1,0:T(8,128)(2,1)} %get-tuple-element.8) | copy-start | bytes 442372
